TPU v7x, 32 devices: a whole 2x2x4 slice. The times are simulated.
32 devices in a mesh: dp: 2 (over core), seq: 8 (over z, y), tensor: 2 (over x).
Axes of the slice: x: 2, y: 2, z: 4, core: 2. Of those that a mesh axis runs over, the one named last changes fastest.
Arguments:
- queries: bfloat16 [4096, 2048], P(('dp', 'seq'), 'tensor'), parts along dimension 0
- routed_key_rows: bfloat16 [4096, 512], P(('dp', 'seq'), 'tensor'), parts along dimension 0
- routed_value_rows: bfloat16 [4096, 512], P(('dp', 'seq'), 'tensor'), parts along dimension 0, may hold values from -6 to 6
- grad_out: bfloat16 [4096, 2048], P(('dp', 'seq'), 'tensor'), parts along dimension 0, may hold values from -6 to 6
- gate_logit: float32 [4096], P(('dp', 'seq')), parts along dimension 0, may hold values from -6 to 6
- block_ids: int32 [16, 2], P('dp'), parts along dimension 0, may hold values from 0 to 15, as said below
- block_counts: int32 [16], P('dp'), parts along dimension 0, may hold values from 1 to 2, as said below
Outputs:
- query_grads: bfloat16 [4096, 2048], P(('dp', 'seq'), 'tensor'), parts along dimension 0
- key_grads: bfloat16 [4096, 512], P(('dp', 'seq'), 'tensor'), parts along dimension 0
- value_grads: bfloat16 [4096, 512], P(('dp', 'seq'), 'tensor'), parts along dimension 0
- gate_grads: float32 [4096], P(('dp', 'seq')), parts along dimension 0
There are 2 independent parts, one for each index of `dp`. A program takes and returns all parts, laid end to end along the dimension named above; each array names one. Nothing has to cross between parts.
Inputs may be any that keep to these rules, and one draw needn't show every extreme that they name: `block_ids`: within each shard the routed block positions are distinct. Only the first block_counts[s] slots of shard s hold routed blocks; the rows of the other slots are not live.
All inputs are finite; a program needn't handle non-finite values.
Results may differ from a plain program's by a relative error of at most 0.028.
Values may be sent and summed in bfloat16 or wider, within the bound.
A program may use at most 128 MiB of HBM per device.

v0:
```python
import math

import jax
import jax.numpy as jnp
from jax import lax
from jax.sharding import PartitionSpec as P

HEAD_SIZE = 128
QUERY_HEADS = 16
KEY_VALUE_HEADS = 4
BLK = 128
SPAN_BLK = 16


def token_positions(block_ids, block_counts):
    shard_count, slot_count = block_ids.shape
    shard_index = jnp.arange(shard_count, dtype=jnp.int32)[:, None]
    block_start = (shard_index * SPAN_BLK + block_ids) * BLK
    offsets = jnp.arange(BLK, dtype=jnp.int32)
    positions = (block_start[:, :, None] + offsets[None, None, :]).reshape(-1)
    slot_live = jnp.arange(slot_count, dtype=jnp.int32)[None, :] < block_counts[:, None]
    live_rows = jnp.broadcast_to(slot_live[:, :, None], (shard_count, slot_count, BLK)).reshape(-1)
    return (positions, live_rows)


def local(
    queries, routed_key_rows, routed_value_rows, grad_out, gate_logit, block_ids, block_counts
):
    row_count = queries.shape[0]
    key_width = routed_key_rows.shape[1]
    kv_local = key_width // HEAD_SIZE
    query_group_width = QUERY_HEADS // KEY_VALUE_HEADS
    seq_index = lax.axis_index("seq")
    key_total = lax.axis_size("seq") * row_count
    score_scale = HEAD_SIZE ** (-0.5)
    positions, live_rows = token_positions(block_ids, block_counts)
    first_row = seq_index * row_count
    query_pos = lax.dynamic_slice_in_dim(positions, first_row, row_count)
    query_live = lax.dynamic_slice_in_dim(live_rows, first_row, row_count)
    query_rows = first_row + jnp.arange(row_count, dtype=jnp.int32)
    last_row = first_row + row_count - 1
    block_target = row_count * max(1, 512 // row_count)
    gate_value = jax.nn.sigmoid(gate_logit)
    output_gradients = (gate_value[:, None] * grad_out.astype(jnp.float32)).astype(jnp.bfloat16)
    heads_of_queries = queries.reshape(row_count, kv_local, query_group_width, HEAD_SIZE)
    output_gradient_heads = output_gradients.reshape(
        row_count, kv_local, query_group_width, HEAD_SIZE
    )

    def block_scores(key_block, block_first):
        block_rows = key_block.shape[0]
        heads_of_keys = key_block.reshape(block_rows, kv_local, HEAD_SIZE)
        scores = (
            jnp.einsum(
                "rkgd,jkd->kgrj",
                heads_of_queries,
                heads_of_keys,
                preferred_element_type=jnp.float32,
            )
            * score_scale
        )
        key_pos = lax.dynamic_slice_in_dim(positions, block_first, block_rows)
        key_live = lax.dynamic_slice_in_dim(live_rows, block_first, block_rows)
        key_index = block_first + jnp.arange(block_rows, dtype=jnp.int32)
        allowed = key_live[None, :] & (key_pos[None, :] <= query_pos[:, None]) | (
            key_index[None, :] == query_rows[:, None]
        )
        return (scores, allowed, heads_of_keys)

    def grads_against(value_block):
        heads_of_values = value_block.reshape(value_block.shape[0], kv_local, HEAD_SIZE)
        return jnp.einsum(
            "rkgd,jkd->kgrj",
            output_gradient_heads,
            heads_of_values,
            preferred_element_type=jnp.float32,
        )

    def stats_block(state_now, key_block, value_block, block_first):
        row_max, row_total, weighted = state_now
        scores, allowed, heads_of_keys = block_scores(key_block, block_first)
        block_max = jnp.max(jnp.where(allowed, scores, -jnp.inf), axis=-1)
        new_max = jnp.maximum(row_max, block_max)
        weights = jnp.where(allowed, jnp.exp(scores - new_max[..., None]), 0.0)
        prob_grads = grads_against(value_block)
        rescale = jnp.exp(row_max - new_max)
        return (
            new_max,
            row_total * rescale + jnp.sum(weights, axis=-1),
            weighted * rescale + jnp.sum(weights * prob_grads, axis=-1),
        )

    def over_blocks(block_fn, state_now, key_piece, value_piece):
        piece_rows = key_piece.shape[0]
        sub_rows = math.gcd(piece_rows, block_target)

        def one_turn(turn_index, carried):
            offset = turn_index * sub_rows
            key_block = lax.dynamic_slice_in_dim(key_piece, offset, sub_rows)
            value_block = lax.dynamic_slice_in_dim(value_piece, offset, sub_rows)

            def compute(inner_state):
                return block_fn(inner_state, key_block, value_block, offset)

            def keep_state(inner_state):
                return inner_state

            return lax.cond(offset <= last_row, compute, keep_state, carried)

        return lax.fori_loop(0, piece_rows // sub_rows, one_turn, state_now)

    stat_shape = (kv_local, query_group_width, row_count)
    stats_seed = (
        jnp.full(stat_shape, -1e30, jnp.float32),
        jnp.zeros(stat_shape, jnp.float32),
        jnp.zeros(stat_shape, jnp.float32),
    )
    pieces = (
        lax.all_gather(routed_key_rows, "seq", axis=0, tiled=True),
        lax.all_gather(routed_value_rows, "seq", axis=0, tiled=True),
    )
    folded = over_blocks(stats_block, stats_seed, pieces[0], pieces[1])
    row_max, row_total, weighted = folded
    live_mask = query_live.astype(jnp.float32)
    delta_rows = weighted / row_total * live_mask
    delta_sum = lax.psum(jnp.sum(delta_rows, axis=(0, 1)), "tensor")
    gate_grads = (1.0 - gate_value) * delta_sum

    def block_terms(key_block, value_block, block_first):
        scores, allowed, heads_of_keys = block_scores(key_block, block_first)
        visible = allowed & query_live[:, None]
        probabilities = (
            jnp.where(visible, jnp.exp(scores - row_max[..., None]), 0.0) / row_total[..., None]
        )
        prob_grads = grads_against(value_block)
        score_gradients = (
            probabilities * (prob_grads - delta_rows[..., None]) * score_scale
        ).astype(jnp.bfloat16)
        return (probabilities.astype(jnp.bfloat16), score_gradients, heads_of_keys)

    def key_block_grads(probability_reduced, score_gradients):
        block_rows = score_gradients.shape[-1]
        key_grad = jnp.einsum(
            "fimw,mfiy->wfy", score_gradients, heads_of_queries, preferred_element_type=jnp.float32
        ).reshape(block_rows, key_width)
        value_grad = jnp.einsum(
            "fimw,mfiy->wfy",
            probability_reduced,
            output_gradient_heads,
            preferred_element_type=jnp.float32,
        ).reshape(block_rows, key_width)
        return (key_grad, value_grad)

    def full_block(state_now, key_block, value_block, block_first):
        query_grad, key_sums, value_sums = state_now
        probability_reduced, score_gradients, heads_of_keys = block_terms(
            key_block, value_block, block_first
        )
        query_grad = query_grad + jnp.einsum(
            "kgrj,jkd->rkgd", score_gradients, heads_of_keys, preferred_element_type=jnp.float32
        )
        key_grad, value_grad = key_block_grads(probability_reduced, score_gradients)
        key_sums = lax.dynamic_update_slice_in_dim(key_sums, key_grad, block_first, 0)
        value_sums = lax.dynamic_update_slice_in_dim(value_sums, value_grad, block_first, 0)
        return (query_grad, key_sums, value_sums)

    grad_seed = jnp.zeros((row_count, kv_local, query_group_width, HEAD_SIZE), jnp.float32)
    partial_seed = (
        grad_seed,
        jnp.zeros((key_total, key_width), jnp.float32),
        jnp.zeros((key_total, key_width), jnp.float32),
    )
    pieces = (
        lax.all_gather(routed_key_rows, "seq", axis=0, tiled=True),
        lax.all_gather(routed_value_rows, "seq", axis=0, tiled=True),
    )
    query_grad, key_sums, value_sums = over_blocks(full_block, partial_seed, pieces[0], pieces[1])
    key_own, value_own = (
        lax.psum_scatter(
            key_sums.astype(jnp.bfloat16), "seq", scatter_dimension=0, tiled=True
        ).astype(jnp.float32),
        lax.psum_scatter(
            value_sums.astype(jnp.bfloat16), "seq", scatter_dimension=0, tiled=True
        ).astype(jnp.float32),
    )
    return (
        query_grad.reshape(row_count, kv_local * query_group_width * HEAD_SIZE).astype(
            jnp.bfloat16
        ),
        key_own.astype(jnp.bfloat16),
        value_own.astype(jnp.bfloat16),
        gate_grads,
    )


def solution(mesh):
    in_specs = (
        P(("dp", "seq"), "tensor"),
        P(("dp", "seq"), "tensor"),
        P(("dp", "seq"), "tensor"),
        P(("dp", "seq"), "tensor"),
        P(("dp", "seq")),
        P("dp", None),
        P("dp"),
    )
    out_specs = (
        P(("dp", "seq"), "tensor"),
        P(("dp", "seq"), "tensor"),
        P(("dp", "seq"), "tensor"),
        P(("dp", "seq")),
    )
    return jax.shard_map(local, mesh=mesh, in_specs=in_specs, out_specs=out_specs, check_vma=False)
```

profile of v0, /device:TPU:0, one launch (start us, length us, event | category | flops | bytes accessed | tf_op | source)
XLA Modules:
  0.0 285.6 jit_solution(7243535389360933397)
XLA Ops:
  7.2 1.7 copy.62
  9.0 1.7 copy.64
  13.0 1.2 multiply_convert_fusion
  15.5 37.4 %all-gather.3.cloned.1.call-done = bf16[2048,256]{0,1:T(8,128)(2,1)} async-done(((bf16[256,256]{0,1:T(8,128)(2,1)}), bf16[2048,256]{0,1:T(8,128)(2,1)}) %all-gather.3.cloned.1.call-update) | async-done | bytes 1048592 | tf_op jit(solution)/shard_map/all_gather | solution.py:174
  52.9 41.1 %all-gather.5.cloned.1.call-done = bf16[2048,256]{0,1:T(8,128)(2,1)} async-done(((bf16[256,256]{0,1:T(8,128)(2,1)}), bf16[2048,256]{0,1:T(8,128)(2,1)}) %all-gather.5.cloned.1.call-update) | async-done | bytes 1048592 | tf_op jit(solution)/shard_map/all_gather | solution.py:175
  94.0 5.2 %while.36 = (s32[]{:T(128)}, f32[2,4,256]{2,1,0:T(4,128)S(1)}, f32[2,4,256]{2,1,0:T(4,128)S(1)}, f32[2,4,256]{2,1,0:T(4,128)S(1)}, s32[]{:T(128)}, /*index=5*/s3...) while((s32[]{:T(128)}, f32[2,4,256]{2,1,0:T(4,128)S(1)}, ...), condition=%wide.region_6.7_spmd.clone, body=%wide.region_0.6_spmd.clone.sunk | while | flops 549987072 | bytes 15907789 | solution.py:110
  94.1 4.8 %conditional.6 = ((f32[2,4,256]{2,1,0:T(4,128)S(1)}, f32[2,4,256]{2,1,0:T(4,128)S(1)}, f32[2,4,256]{2,1,0:T(4,128)S(1)})) conditional(s32[]{:T(128)} %convert_element_type.68, (f32[2,4,256]{2,1,0:T(4,128)S(1)}, f32[2,4,256]{2,1,0:T(4,128)S(1)}, f32[2,4,256]{2,1,0:T(4,128)S(1)}) %tuple.110, (s32[]{:T(128)}, pred[8,2]{1,0:T(8,128)(4,1)S(1)}, ...), branch_computations={%region_1.0_spmd, %region_2.5_spmd} | conditional | flops 549985024 | bytes 15898214 | solution.py:108
  94.3 1.1 constant_dynamic-slice_fusion
  95.7 0.9 fusion.13
  96.6 1.4 fusion.12
  98.0 0.9 fusion.16
  99.3 1.1 broadcast.84
  100.5 8.7 %while.37 = (s32[]{:T(128)}, f32[256,2,4,128]{3,0,2,1:T(8,128)S(1)}, bf16[2048,256]{0,1:T(8,128)(2,1)}, bf16[2048,256]{0,1:T(8,128)(2,1)S(1)}, s32[]{:T(128)}, /...) while((s32[]{:T(128)}, ...), condition=%wide.region_10.0_spmd.clone, body=%wide.region_7.10_spmd.clone.sunk | while | flops 1352534784 | bytes 26795284 | solution.py:110
  100.6 8.3 %conditional.7 = ((f32[256,2,4,128]{3,0,2,1:T(8,128)S(1)}, bf16[2048,256]{0,1:T(8,128)(2,1)}, bf16[2048,256]{0,1:T(8,128)(2,1)S(1)})) conditional(s32[]{:T(128)} %convert_element_type.69, (f32[256,2,4,128]{3,0,2,1:T(8,128)S(1)}, bf16[2048,256]{0,1:T(8,128)(2,1)}, bf16[2048,256]{0,1:T(8,128)(2,1)S(1)}) %tuple.113, (s32[]{:T(128)}, ...), branch_computations={%region_8.8_spmd, %region_9.9_spmd} | conditional | flops 1352532736 | bytes 26785646 | solution.py:108
  101.1 1.0 constant_dynamic-slice_fusion.3
  102.1 1.0 constant_dynamic-slice_fusion.2
  103.1 1.3 fusion.22
  106.8 1.3 fusion.25
  109.1 1.3 copy.70
  110.6 2.3 copy.69
  113.3 1.2 convert_element_type.55
  114.5 4.9 %psum.7 = f32[256]{0:T(256)S(1)} all-reduce(f32[256]{0:T(256)S(1)} %get-tuple-element.1025), channel_id=1, replica_groups=mesh['dp'=2,'seq'=8,'tensor'=2] {'tensor'}, use_global_device_ids=true, to_apply=%region_14.15 | all-reduce | flops 256 | bytes 2048 | tf_op jit(solution)/shard_map/psum | solution.py:126
  120.0 92.4 %reduce-scatter.5.cloned.1.call-done = bf16[256,256]{1,0:T(8,128)(2,1)} async-done(((bf16[2048,256]{1,0:T(8,128)(2,1)}), bf16[256,256]{1,0:T(8,128)(2,1)}) %reduce-scatter.5.cloned.1.call-update) | async-done | bytes 131088 | tf_op jit(solution)/shard_map/reduce_scatter | solution.py:182
  212.4 66.6 %reduce-scatter.3.cloned.1.call-done = bf16[256,256]{1,0:T(8,128)(2,1)} async-done(((bf16[2048,256]{1,0:T(8,128)(2,1)}), bf16[256,256]{1,0:T(8,128)(2,1)}) %reduce-scatter.3.cloned.1.call-update) | async-done | bytes 131088 | tf_op jit(solution)/shard_map/reduce_scatter | solution.py:179
  (78 shorter events, 10.0 us)
Async XLA Ops:
  7.2 7.6 %copy-start = (bf16[256,1024]{1,0:T(8,128)(2,1)S(1)}, bf16[256,1024]{1,0:T(8,128)(2,1)}, u32[]{:S(2)}) copy-start(bf16[256,1024]{1,0:T(8,128)(2,1)} %param.15) | copy-start | bytes 1572868
  7.2 45.7 %all-gather.3.cloned.1.call-start = ((), (), s32[]{:S(2)}) async-start(), calls=%async_computation.2 | async-start | bytes 1179648 | tf_op jit(solution)/shard_map/all_gather | solution.py:174
  9.0 85.0 %all-gather.5.cloned.1.call-start = ((), (), s32[]{:S(2)}) async-start(), calls=%async_computation.3 | async-start | bytes 1179648 | tf_op jit(solution)/shard_map/all_gather | solution.py:175
  10.7 201.7 %reduce-scatter.5.cloned.1.call-start = ((), (), s32[]{:S(2)}) async-start(), calls=%async_computation.5 | async-start | bytes 1179648 | tf_op jit(solution)/shard_map/reduce_scatter | solution.py:182
  110.5 8.9 %copy-start.1 = (f32[256]{0:T(256)S(1)}, f32[256]{0:T(256)}, u32[]{:S(2)}) copy-start(f32[256]{0:T(256)} %param.19) | copy-start | bytes 3076
  110.5 168.5 %reduce-scatter.3.cloned.1.call-start = ((), (), s32[]{:S(2)}) async-start(), calls=%async_computation.4 | async-start | bytes 1179648 | tf_op jit(solution)/shard_map/reduce_scatter | solution.py:179
Sparse Core Ops, SparseCore 0:
  10.6 42.2 all-gather.2
  55.5 38.4 all-gather.4
  110.6 101.7 reduce-scatter.4
  216.6 62.3 reduce-scatter.2
where the time goes:
time: 286 us
  waiting for transfers between devices  238 us (83%)
  local copies, waits for them, and re-layouts  16.1 us (6%)
  between operations  13.8 us (5%)
  matrix products  7.24 us (3%)
  other arithmetic  5.57 us (2%)
  blocking collectives  4.91 us (2%)
    reduce_scatter x1, waiting for transfers between devices, local(): lax.psum_scatter(value_sums.astype(jnp.bfloat16), 'seq', scatter_dimensio...  92.4 us
    reduce_scatter x1, waiting for transfers between devices, local(): lax.psum_scatter(key_sums.astype(jnp.bfloat16), 'seq', scatter_dimension=...  66.6 us
    all_gather x1, waiting for transfers between devices, local(): lax.all_gather(routed_value_rows, 'seq', axis=0, tiled=True)  41.1 us
    all_gather x1, waiting for transfers between devices, local(): lax.all_gather(routed_key_rows, 'seq', axis=0, tiled=True)  37.4 us
  transfers between devices with their start and end apart: 4, of which 4 were waited for; matrix products, arithmetic and copies ran while one was open for 4% of the time, Pallas kernels for 0%

commit v1 on v0

v1 whole, which is shorter than its diff:
```python
import functools
import math

import jax
import jax.numpy as jnp
from jax import lax
from jax.experimental import pallas as pl
from jax.experimental.pallas import tpu as pltpu
from jax.sharding import PartitionSpec as P

D = 128
GROUP = 4
BLK = 128
SCALE = D ** -0.5
EXP2_SCALE = SCALE * math.log2(math.e)
MESH = pl.DeviceIdType.MESH
F32 = jnp.float32
BF16 = jnp.bfloat16


def mm(a, b):
    return jnp.dot(a, b, preferred_element_type=F32)


def kernel(
    n, kv_heads,
    ids_ref, counts_ref, q_ref, k_ref, v_ref, go_ref, gate_ref,
    dq_ref, dk_ref, dv_ref, dgate_ref,
    kv, qn, qt, on, ot, exps, block_max, row_max, row_sum, row_dot, delta, factor,
    dqt, own, bias, ysend, yrecv, zsend, zrecv, tsend, trecv,
    kv_sem, up_sem, across_sem, ysend_sem, yrecv_sem, zsend_sem, zrecv_sem, t_sem,
):
    rows = q_ref.shape[0]
    me = lax.axis_index("seq")
    tensor = lax.axis_index("tensor")
    half = n // 2
    z, y = me // 2, me % 2
    partner = 2 * z + (1 - y)

    def up_copy(g, zd):
        return pltpu.make_async_remote_copy(
            kv.at[g, me], kv.at[g, me], up_sem.at[g, zd], kv_sem.at[g, me],
            device_id={"seq": 2 * zd + y}, device_id_type=MESH)

    def across_copy(g, zz):
        b = 2 * zz + y
        return pltpu.make_async_remote_copy(
            kv.at[g, b], kv.at[g, b], across_sem.at[g, zz], kv_sem.at[g, b],
            device_id={"seq": partner}, device_id_type=MESH)

    def arrived(g, b):
        pltpu.make_async_remote_copy(
            kv.at[g, b], kv.at[g, b], up_sem.at[g, 0], kv_sem.at[g, b],
            device_id={"seq": partner}, device_id_type=MESH).wait_recv()

    def ygrad_copy(g, zz):
        return pltpu.make_async_remote_copy(
            ysend.at[g, zz], yrecv.at[g, zz], ysend_sem.at[g, zz], yrecv_sem.at[g, zz],
            device_id={"seq": partner}, device_id_type=MESH)

    def zgrad_copy(g, zz):
        return pltpu.make_async_remote_copy(
            zsend.at[g, zz], zrecv.at[g, z], zsend_sem.at[g, zz], zrecv_sem.at[g, z],
            device_id={"seq": 2 * zz + y}, device_id_type=MESH)

    def zgrad_arrived(g, zs):
        pltpu.make_async_remote_copy(
            zsend.at[g, zs], zrecv.at[g, zs], zsend_sem.at[g, zs], zrecv_sem.at[g, zs],
            device_id={"seq": partner}, device_id_type=MESH).wait_recv()

    def tensor_copy():
        return pltpu.make_async_remote_copy(
            tsend, trecv, t_sem.at[0], t_sem.at[1],
            device_id={"tensor": 1 - tensor}, device_id_type=MESH)

    def loop(lo, hi, body):
        def step(i, carry):
            body(i)
            return carry
        lax.fori_loop(lo, hi, step, 0)

    barrier = pltpu.get_barrier_semaphore()
    pl.semaphore_signal(barrier, inc=1, device_id={"seq": partner}, device_id_type=MESH)
    pl.semaphore_signal(barrier, inc=1, device_id={"tensor": 1 - tensor}, device_id_type=MESH)

    def greet(step):
        other = lax.rem(z + step, half)
        pl.semaphore_signal(barrier, inc=1, device_id={"seq": 2 * other + y}, device_id_type=MESH)
    loop(1, half, greet)

    for g in range(kv_heads):
        kv[g, me, 0] = k_ref[:, g * D:(g + 1) * D]
        kv[g, me, 1] = v_ref[:, g * D:(g + 1) * D]
    pl.semaphore_wait(barrier, half + 1)

    def send_own(g):
        @pl.when(y == 0)
        def _():
            across_copy(g, z).start()
        loop(z + 1, half, lambda zd: up_copy(g, zd).start())

    send_own(0)

    gate = 1.0 / (1.0 + jnp.exp(-gate_ref[...]))
    gate_columns = jnp.transpose(jnp.broadcast_to(gate, (D, rows)))
    for g in range(kv_heads):
        for h in range(GROUP):
            source = slice((g * GROUP + h) * D, (g * GROUP + h + 1) * D)
            at = slice(h * rows, (h + 1) * rows)
            out_grad = (gate_columns * go_ref[:, source].astype(F32)).astype(BF16)
            on[g, at, :] = out_grad
            ot[g, :, at] = jnp.transpose(out_grad)
            qn[g, at, :] = q_ref[:, source]
            qt[g, :, at] = jnp.transpose(q_ref[:, source])

    def by_slot(index, first, second):
        return jnp.where(index < BLK, first, second)

    key_row = lax.broadcasted_iota(jnp.int32, (rows, rows), 0)
    query_row = lax.broadcasted_iota(jnp.int32, (rows, rows), 1)
    id0, id1, count = ids_ref[me, 0], ids_ref[me, 1], counts_ref[me]
    key_pos = by_slot(key_row, id0 * BLK, id1 * BLK - BLK) + key_row
    query_pos = by_slot(query_row, id0 * BLK, id1 * BLK - BLK) + query_row
    key_slot = by_slot(key_row, 0, 1)
    allowed = ((key_slot < count) & (key_pos <= query_pos)) | (key_row == query_row)
    bias[...] = jnp.where(allowed, 0.0, -jnp.inf).astype(F32)
    query_slot = by_slot(lax.broadcasted_iota(jnp.int32, (1, rows), 1), 0, 1)
    live = jnp.where(query_slot < count, 1.0, 0.0).astype(F32)

    def first_pass(g, b, is_own):
        keys, values = kv[g, b, 0], kv[g, b, 1]
        shut0 = jnp.where(counts_ref[b] > 0, 0.0, -jnp.inf).astype(F32)
        shut1 = jnp.where(counts_ref[b] > 1, 0.0, -jnp.inf).astype(F32)
        for h in range(GROUP):
            at = slice(h * rows, (h + 1) * rows)
            s = mm(keys, qt[g, :, at])
            if is_own:
                s = s + bias[...]
            else:
                s = jnp.concatenate([s[:BLK] + shut0, s[BLK:] + shut1], axis=0)
            prob_grads = mm(values, ot[g, :, at])
            top = jnp.max(s, axis=0, keepdims=True)
            if not is_own:
                before = row_max[:, at]
                top = jnp.maximum(before, top)
            e = jnp.exp2((s - top) * EXP2_SCALE)
            total = jnp.sum(e, axis=0, keepdims=True)
            dot = jnp.sum(e * prob_grads, axis=0, keepdims=True)
            if not is_own:
                shrink = jnp.exp2((before - top) * EXP2_SCALE)
                total = total + row_sum[:, at] * shrink
                dot = dot + row_dot[:, at] * shrink
            row_max[:, at] = top
            row_sum[:, at] = total
            row_dot[:, at] = dot
            block_max[b, :, at] = top
            exps[b, :, at] = e.astype(BF16)

    def gather(g):
        first_pass(g, me, True)

        @pl.when(y == 1)
        def _():
            arrived(g, partner)
            first_pass(g, partner, False)

        def step(k):
            zz = z - k
            same, other = 2 * zz + y, 2 * zz + 1 - y
            arrived(g, same)
            across_copy(g, zz).start()
            first_pass(g, same, False)
            arrived(g, other)
            first_pass(g, other, False)
        loop(1, z + 1, step)

    def close_stats(g):
        for h in range(GROUP):
            at = slice(h * rows, (h + 1) * rows)
            inverse = live / row_sum[:, at]
            delta[:, at] = row_dot[:, at] * inverse
            factor[:, at] = inverse
        dqt[...] = jnp.zeros_like(dqt)

    def second_pass(g, b):
        keys, values = kv[g, b, 0], kv[g, b, 1]
        keys_t = jnp.transpose(keys)
        dk = jnp.zeros((rows, D), F32)
        dv = jnp.zeros((rows, D), F32)
        for h in range(GROUP):
            at = slice(h * rows, (h + 1) * rows)
            weight = jnp.exp2((block_max[b, :, at] - row_max[:, at]) * EXP2_SCALE) * factor[:, at]
            probs = exps[b, :, at].astype(F32) * weight
            prob_grads = mm(values, ot[g, :, at])
            score_grads = (probs * (prob_grads - delta[:, at])).astype(BF16)
            dv = dv + mm(probs.astype(BF16), on[g, at, :])
            dk = dk + mm(score_grads, qn[g, at, :])
            dqt[:, at] += mm(keys_t, score_grads)
        return dk * SCALE, dv

    def grads(g):
        def to_partner(zz):
            dk, dv = second_pass(g, 2 * zz + 1 - y)
            ysend[g, zz, 0] = dk.astype(BF16)
            ysend[g, zz, 1] = dv.astype(BF16)
            ygrad_copy(g, zz).start()

        def keep(zz):
            dk, dv = second_pass(g, 2 * zz + y)
            own[g, zz, 0] = dk
            own[g, zz, 1] = dv

        loop(0, z + y, to_partner)
        loop(0, z + 1, keep)
        for h in range(GROUP):
            at = slice(h * rows, (h + 1) * rows)
            target = slice((g * GROUP + h) * D, (g * GROUP + h + 1) * D)
            dq_ref[:, target] = jnp.transpose(dqt[:, at] * SCALE).astype(BF16)

    def to_owners(g):
        def step(zz):
            ygrad_copy(g, zz).wait_recv()
            zsend[g, zz] = (own[g, zz] + yrecv[g, zz].astype(F32)).astype(BF16)
            zgrad_copy(g, zz).start()
        loop(0, z, step)

    def finish(g):
        @pl.when(y == 0)
        def _():
            ygrad_copy(g, z).wait_recv()
            own[g, z] = own[g, z] + yrecv[g, z].astype(F32)

        def step(zs):
            zgrad_arrived(g, zs)
            own[g, z] = own[g, z] + zrecv[g, zs].astype(F32)
        loop(z + 1, half, step)
        dk_ref[:, g * D:(g + 1) * D] = own[g, z, 0].astype(BF16)
        dv_ref[:, g * D:(g + 1) * D] = own[g, z, 1].astype(BF16)

    delta_sum = jnp.zeros((1, rows), F32)
    for g in range(kv_heads):
        gather(g)
        if g + 1 < kv_heads:
            send_own(g + 1)
        close_stats(g)
        for h in range(GROUP):
            delta_sum = delta_sum + delta[:, h * rows:(h + 1) * rows]
        if g + 1 == kv_heads:
            tsend[...] = jnp.broadcast_to(delta_sum, tsend.shape)
            tensor_copy().start()
        if g > 0:
            to_owners(g - 1)
        grads(g)
    to_owners(kv_heads - 1)
    tensor_copy().wait_recv()
    dgate_ref[...] = (1.0 - gate) * (delta_sum + trecv[0:1, :])
    for g in range(kv_heads):
        finish(g)

    tensor_copy().wait_send()
    for g in range(kv_heads):
        loop(z + 1, half, lambda zd: up_copy(g, zd).wait_send())
        loop(0, z + 1 - y, lambda zz: across_copy(g, zz).wait_send())
        loop(0, z + y, lambda zz: ygrad_copy(g, zz).wait_send())
        loop(0, z, lambda zz: zgrad_copy(g, zz).wait_send())


def local(n, queries, keys, values, grad_out, gate_logit, block_ids, block_counts):
    rows, width = queries.shape
    kv_width = keys.shape[1]
    kv_heads = kv_width // D
    half = n // 2
    group_rows = GROUP * rows
    vmem = pl.BlockSpec(memory_space=pltpu.VMEM)
    smem = pl.BlockSpec(memory_space=pltpu.SMEM)
    pair = (2, rows, D)
    sem = pltpu.SemaphoreType.DMA
    dq, dk, dv, dgate = pl.pallas_call(
        functools.partial(kernel, n, kv_heads),
        out_shape=(
            jax.ShapeDtypeStruct((rows, width), BF16),
            jax.ShapeDtypeStruct((rows, kv_width), BF16),
            jax.ShapeDtypeStruct((rows, kv_width), BF16),
            jax.ShapeDtypeStruct((1, rows), F32),
        ),
        in_specs=[smem, smem, vmem, vmem, vmem, vmem, vmem],
        out_specs=(vmem, vmem, vmem, vmem),
        scratch_shapes=[
            pltpu.VMEM((kv_heads, n) + pair, BF16),
            pltpu.VMEM((kv_heads, group_rows, D), BF16),
            pltpu.VMEM((kv_heads, D, group_rows), BF16),
            pltpu.VMEM((kv_heads, group_rows, D), BF16),
            pltpu.VMEM((kv_heads, D, group_rows), BF16),
            pltpu.VMEM((n, rows, group_rows), BF16),
            pltpu.VMEM((n, 1, group_rows), F32),
            pltpu.VMEM((1, group_rows), F32),
            pltpu.VMEM((1, group_rows), F32),
            pltpu.VMEM((1, group_rows), F32),
            pltpu.VMEM((1, group_rows), F32),
            pltpu.VMEM((1, group_rows), F32),
            pltpu.VMEM((D, group_rows), F32),
            pltpu.VMEM((kv_heads, half) + pair, F32),
            pltpu.VMEM((rows, rows), F32),
            pltpu.VMEM((kv_heads, half) + pair, BF16),
            pltpu.VMEM((kv_heads, half) + pair, BF16),
            pltpu.VMEM((kv_heads, half) + pair, BF16),
            pltpu.VMEM((kv_heads, half) + pair, BF16),
            pltpu.VMEM((8, rows), F32),
            pltpu.VMEM((8, rows), F32),
            sem((kv_heads, n)),
            sem((kv_heads, half)),
            sem((kv_heads, half)),
            sem((kv_heads, half)),
            sem((kv_heads, half)),
            sem((kv_heads, half)),
            sem((kv_heads, half)),
            sem((2,)),
        ],
        compiler_params=pltpu.CompilerParams(
            collective_id=0, has_side_effects=True, vmem_limit_bytes=60 * 1024 * 1024
        ),
        cost_estimate=pl.CostEstimate(
            flops=12 * n * rows * rows * width,
            bytes_accessed=6 * rows * (width + kv_width),
            transcendentals=n * rows * rows * width // D,
        ),
        name="mod_attention_grads",
    )(block_ids, block_counts, queries, keys, values, grad_out, gate_logit.reshape(1, rows))
    return dq, dk, dv, dgate.reshape(rows)


def solution(mesh):
    in_specs = (
        P(("dp", "seq"), "tensor"),
        P(("dp", "seq"), "tensor"),
        P(("dp", "seq"), "tensor"),
        P(("dp", "seq"), "tensor"),
        P(("dp", "seq")),
        P("dp", None),
        P("dp"),
    )
    out_specs = (
        P(("dp", "seq"), "tensor"),
        P(("dp", "seq"), "tensor"),
        P(("dp", "seq"), "tensor"),
        P(("dp", "seq")),
    )
    return jax.shard_map(
        functools.partial(local, mesh.shape["seq"]),
        mesh=mesh, in_specs=in_specs, out_specs=out_specs, check_vma=False,
    )
```

time: 286 us -> 82.7 us (0.29)
  waiting for transfers between devices: 238 us -> 0 us
  Pallas kernels: 0 us -> 76.4 us
  between operations: 13.8 us -> 0.66 us
  local copies, waits for them, and re-layouts: 16.1 us -> 5.42 us
  matrix products: 7.24 us -> 0 us
  other arithmetic: 5.57 us -> 0 us
  blocking collectives: 4.91 us -> 0 us
    reduce_scatter x2 -> x0, waiting for transfers between devices: 159 us -> none  [the longest x1 92.4 us: local(): lax.psum_scatter(value_sums.astype(jnp.bfloat16), 'seq', scatter_dimensio...]
    all_gather x2 -> x0, waiting for transfers between devices: 78.4 us -> none  [the longest x1 41.1 us: local(): lax.all_gather(routed_value_rows, 'seq', axis=0, tiled=True)]
    pallas_call x0 -> x1, Pallas kernels: none -> 76.4 us  [local(): pl.pallas_call(functools.partial(kernel, n, kv_heads), out_shape=(jax.Sha...]
    dot_general x7 -> x0, matrix products: 7.24 us -> none  [the longest x2 2.18 us: grads_against(): jnp.einsum('rkgd,jkd->kgrj', output_gradient_heads, heads_of_values, pref...]
    psum x1 -> x0, blocking collectives: 4.91 us -> none  [local(): delta_sum = lax.psum(jnp.sum(delta_rows, axis=(0, 1)), 'tensor')]
    while x2 -> x0, local copies, waits for them, and re-layouts: 3.59 us -> none  [over_blocks(): return lax.fori_loop(0, piece_rows // sub_rows, one_turn, state_now)]
    dynamic_slice x8 -> x0, local copies, waits for them, and re-layouts: 3.41 us -> none  [the longest x2 2.04 us: one_turn(): key_block = lax.dynamic_slice_in_dim(key_piece, offset, sub_rows)]
  transfers between devices with their start and end apart: 4 -> 0, of which waited for: 4 -> 0; matrix products, arithmetic and copies ran while one was open for 4% -> 0% of each run, Pallas kernels for 0% -> 0%
where the time goes in v1:
time: 82.7 us; the launch traced here: 82.5 us
  Pallas kernels  76.4 us (92%)
  local copies, waits for them, and re-layouts  5.42 us (7%)
    pallas_call x1, Pallas kernels, local(): pl.pallas_call(functools.partial(kernel, n, kv_heads), out_shape=(jax.Sha...  76.4 us
    unnamed x13, local copies, waits for them, and re-layouts  5.42 us

profile of v1, /device:TPU:0, one launch (start us, length us, event | category | flops | bytes accessed | tf_op | source)
XLA Modules:
  0.0 82.5 jit_solution(16483154298082753918)
XLA Ops:
  0.6 0.0 copy-start.2
  0.6 0.7 copy-done.2
  1.3 0.7 copy.11.ids_ref
  2.0 76.4 %mod_attention_grads.1 = (bf16[256,1024]{1,0:T(8,128)(2,1)}, bf16[256,256]{1,0:T(8,128)(2,1)}, bf16[256,256]{1,0:T(8,128)(2,1)}, f32[1,256]{1,0:T(1,128)}) custom-call(s32[8,2]{1,0:T(8,128)} %copy.11.ids_ref, s32[8]{0:T(128)} %counts_ref.1, bf16[256,1024]{1,0:T(8,128)(2,1)} %q_ref.1, bf16[256,256]{1,0:T(8,128)(2,1)} %k_ref.1, bf16[256,256]{1,0:T(8,128)(2,1)} %v_ref.1, ...), custom_call_target="tpu_custom_call" | custom-call | flops 6442450944 | bytes 1966080 | tf_op jit(solution)/shard_map/mod_attention_grads/pallas_call | solution.py:278
  78.4 0.0 copy-start.1
  78.4 1.9 %copy.16 = bf16[256,1024]{1,0:T(8,128)(2,1)} copy(bf16[256,1024]{1,0:T(8,128)(2,1)} %get-tuple-element.16) | data formatting | bytes 1048576
  80.3 0.0 copy-done.1
  80.3 0.0 copy-start
  80.3 0.7 copy.17
  81.0 0.3 copy-done
  81.3 0.0 copy-start.3
  81.3 0.7 copy.18
  81.9 0.0 copy-done.3
  81.9 0.6 copy.19
Async XLA Ops:
  0.6 0.7 copy-start.2
  78.4 1.9 %copy-start.1 = (bf16[256,256]{1,0:T(8,128)(2,1)S(1)}, bf16[256,256]{1,0:T(8,128)(2,1)}, u32[]{:S(2)}) copy-start(bf16[256,256]{1,0:T(8,128)(2,1)} %get-tuple-element.17) | copy-start | bytes 393220
  80.3 1.0 %copy-start = (bf16[256,256]{1,0:T(8,128)(2,1)S(1)}, bf16[256,256]{1,0:T(8,128)(2,1)}, u32[]{:S(2)}) copy-start(bf16[256,256]{1,0:T(8,128)(2,1)} %get-tuple-element.18) | copy-start | bytes 393220
  81.3 0.7 copy-start.3

commit v2 on v1

v2 whole, which is shorter than its diff:
```python
import functools
import math

import jax
import jax.numpy as jnp
from jax import lax
from jax.experimental import pallas as pl
from jax.experimental.pallas import tpu as pltpu
from jax.sharding import PartitionSpec as P

D = 128
GROUP = 4
BLK = 128
SCALE = D ** -0.5
EXP2_SCALE = SCALE * math.log2(math.e)
MESH = pl.DeviceIdType.MESH
F32 = jnp.float32
BF16 = jnp.bfloat16


def mm(a, b):
    return jnp.dot(a, b, preferred_element_type=F32)


def kernel(
    n,
    ids_ref, counts_ref, q_ref, k_ref, v_ref, go_ref, gate_ref,
    dq_ref, dk_ref, dv_ref, dgate_ref,
    kv, kvx, qx, ox, qn, qt, on, ot, exps, block_max, row_max, row_sum, row_dot, delta, factor,
    dqt, own, bias, low, scored, zsend, zrecv, dqx, dqr, dkvx, dkvr, tsend, trecv,
    kv_sem, up_sem, zsend_sem, zrecv_sem, y_send_sem, y_recv_sem, t_sem,
):
    rows = q_ref.shape[0]
    wide = GROUP * rows
    me = lax.axis_index("seq")
    tensor = lax.axis_index("tensor")
    half = n // 2
    z, y = me // 2, me % 2
    partner = 2 * z + (1 - y)

    def remote(source, target, send_sem, recv_sem, seq):
        return pltpu.make_async_remote_copy(
            source, target, send_sem, recv_sem, device_id={"seq": seq}, device_id_type=MESH)

    def part(p):
        return pl.ds(pl.multiple_of(p * wide, wide), wide)

    def lanes(p, h):
        return pl.ds(pl.multiple_of(p * wide + h * rows, rows), rows)

    def y_copy(i):
        source, target = (
            (kvx, kv.at[me]), (qx, qn.at[part(y)]), (ox, on.at[part(y)]),
            (tsend.at[0], trecv.at[0]), (dqx, dqr), (dkvx, dkvr))[i]
        return remote(source, target, y_send_sem.at[i], y_recv_sem.at[i], partner)

    def up_copy(b, zd):
        return remote(kv.at[b], kv.at[b], up_sem.at[b % 2, zd], kv_sem.at[b], 2 * zd + y)

    def zgrad_copy(zz):
        return remote(zsend.at[zz], zrecv.at[z], zsend_sem.at[zz], zrecv_sem.at[z], 2 * zz + y)

    def tensor_copy():
        return pltpu.make_async_remote_copy(
            tsend.at[1], trecv.at[1], t_sem.at[0], t_sem.at[1],
            device_id={"tensor": 1 - tensor}, device_id_type=MESH)

    def loop(lo, hi, body):
        def step(i, carry):
            body(i)
            return carry
        lax.fori_loop(lo, hi, step, 0)

    def column(g):
        return pl.ds(pl.multiple_of(g * D, D), D)

    barrier = pltpu.get_barrier_semaphore()
    pl.semaphore_signal(barrier, inc=1, device_id={"seq": partner}, device_id_type=MESH)
    pl.semaphore_signal(barrier, inc=1, device_id={"tensor": 1 - tensor}, device_id_type=MESH)

    def greet(step):
        other = lax.rem(z + step, half)
        pl.semaphore_signal(barrier, inc=1, device_id={"seq": 2 * other + y}, device_id_type=MESH)
    loop(1, half, greet)

    kv[me, 0] = k_ref[:, column(y)]
    kv[me, 1] = v_ref[:, column(y)]
    kvx[0] = k_ref[:, column(1 - y)]
    kvx[1] = v_ref[:, column(1 - y)]
    pl.semaphore_wait(barrier, half + 1)
    y_copy(0).start()
    loop(z + 1, half, lambda zd: up_copy(me, half + z - zd).start())

    def head_columns(g, h):
        return pl.ds(pl.multiple_of((g * GROUP + h) * D, D), D)

    for h in range(GROUP):
        qx[h * rows:(h + 1) * rows, :] = q_ref[:, head_columns(1 - y, h)]
    y_copy(1).start()
    gate = 1.0 / (1.0 + jnp.exp(-gate_ref[...]))
    gate_columns = jnp.transpose(jnp.broadcast_to(gate, (D, rows)))

    def gated(g, h):
        return (gate_columns * go_ref[:, head_columns(g, h)].astype(F32)).astype(BF16)

    for h in range(GROUP):
        ox[h * rows:(h + 1) * rows, :] = gated(1 - y, h)
    y_copy(2).start()
    for h in range(GROUP):
        queries, out_grad = q_ref[:, head_columns(y, h)], gated(y, h)
        qn[lanes(y, h), :] = queries
        on[lanes(y, h), :] = out_grad
        qt[:, lanes(y, h)] = jnp.transpose(queries)
        ot[:, lanes(y, h)] = jnp.transpose(out_grad)

    def by_slot(index, first, second):
        return jnp.where(index < BLK, first, second)

    key_row = lax.broadcasted_iota(jnp.int32, (rows, rows), 0)
    query_row = lax.broadcasted_iota(jnp.int32, (rows, rows), 1)
    query_slot = by_slot(lax.broadcasted_iota(jnp.int32, (1, rows), 1), 0, 1)
    key_slot = by_slot(key_row, 0, 1)
    live = []
    for p in range(2):
        b = 2 * z + p
        id0, id1, count = ids_ref[b, 0], ids_ref[b, 1], counts_ref[b]
        key_pos = by_slot(key_row, id0 * BLK, id1 * BLK - BLK) + key_row
        query_pos = by_slot(query_row, id0 * BLK, id1 * BLK - BLK) + query_row
        allowed = ((key_slot < count) & (key_pos <= query_pos)) | (key_row == query_row)
        bias[p] = jnp.where(allowed, 0.0, -jnp.inf).astype(F32)
        live.append(jnp.where(query_slot < count, 1.0, 0.0).astype(F32))

    def first_pass(b, p, is_own):
        keys, values = kv[b, 0], kv[b, 1]
        shut0 = jnp.where(counts_ref[b] > 0, 0.0, -jnp.inf).astype(F32)
        shut1 = jnp.where(counts_ref[b] > 1, 0.0, -jnp.inf).astype(F32)
        for h in range(GROUP):
            at = lanes(p, h)
            s = mm(keys, qt[:, at])
            if is_own:
                s = s + bias[p]
            else:
                s = jnp.concatenate([s[:BLK] + shut0, s[BLK:] + shut1], axis=0)
            prob_grads = mm(values, ot[:, at])
            top = jnp.max(s, axis=0, keepdims=True)
            if not is_own:
                before = row_max[:, at]
                top = jnp.maximum(before, top)
            e = jnp.exp2((s - top) * EXP2_SCALE)
            total = jnp.sum(e, axis=0, keepdims=True)
            dot = jnp.sum(e * prob_grads, axis=0, keepdims=True)
            if not is_own:
                shrink = jnp.exp2((before - top) * EXP2_SCALE)
                total = total + row_sum[:, at] * shrink
                dot = dot + row_dot[:, at] * shrink
            row_max[:, at] = top
            row_sum[:, at] = total
            row_dot[:, at] = dot
            block_max[b, :, at] = top
            exps[b, :, at] = e.astype(BF16)

    y_copy(0).wait_recv()
    loop(z + 1, half, lambda zd: up_copy(partner, half + z - zd).start())
    first_pass(me, y, True)
    y_copy(1).wait_recv()
    y_copy(2).wait_recv()
    for h in range(GROUP):
        qt[:, lanes(1 - y, h)] = jnp.transpose(qn[lanes(1 - y, h), :])
        ot[:, lanes(1 - y, h)] = jnp.transpose(on[lanes(1 - y, h), :])
    first_pass(partner, 1 - y, True)
    first_pass(2 * z, 1, False)

    def gather_step(i):
        b = 2 * z - 1 - i
        remote(kv.at[b], kv.at[b], up_sem.at[0, 0], kv_sem.at[b], partner).wait_recv()
        first_pass(b, 0, False)
        first_pass(b, 1, False)
    loop(0, 2 * z, gather_step)

    sums = []
    for p in range(2):
        total = jnp.zeros((1, rows), F32)
        for h in range(GROUP):
            at = lanes(p, h)
            inverse = live[p] / row_sum[:, at]
            rows_delta = row_dot[:, at] * inverse
            delta[:, at] = rows_delta
            factor[:, at] = inverse
            total = total + rows_delta
        sums.append(total)
    mine = jnp.where(y == 0, sums[0], sums[1])
    tsend[0] = jnp.broadcast_to(jnp.where(y == 0, sums[1], sums[0]), tsend.shape[1:])
    y_copy(3).start()
    dqt[...] = jnp.zeros_like(dqt)

    def score_grads(zz, kb, p):
        b = 2 * zz + kb
        values = kv[b, 1]
        row_at = slice(kb * rows, (kb + 1) * rows)
        for h in range(GROUP):
            at = slice(p * wide + h * rows, p * wide + (h + 1) * rows)
            weight = jnp.exp2((block_max[b, :, at] - row_max[:, at]) * EXP2_SCALE) * factor[:, at]
            probs = exps[b, :, at].astype(F32) * weight
            prob_grads = mm(values, ot[:, at])
            low[row_at, at] = probs.astype(BF16)
            scored[row_at, at] = (probs * (prob_grads - delta[:, at])).astype(BF16)

    def key_value_grads(kb, first):
        row_at = slice(kb * rows, (kb + 1) * rows)
        dk = mm(scored[row_at, first:], qn[first:, :]) * SCALE
        dv = mm(low[row_at, first:], on[first:, :])
        return dk, dv

    def add_query_grads(zz, key_blocks, p):
        keys_t = jnp.concatenate([jnp.transpose(kv[2 * zz + kb, 0]) for kb in key_blocks], axis=1)
        for h in range(0, GROUP, 2):
            at = slice(p * wide + h * rows, p * wide + (h + 2) * rows)
            dqt[:, at] += mm(keys_t, scored[:len(key_blocks) * rows, at])

    def pair_step(zz):
        for kb in range(2):
            for p in range(2):
                score_grads(zz, kb, p)
            dk, dv = key_value_grads(kb, 0)
            zsend[zz, kb, 0] = dk.astype(BF16)
            zsend[zz, kb, 1] = dv.astype(BF16)
        zgrad_copy(zz).start()
        for p in range(2):
            add_query_grads(zz, (0, 1), p)
    loop(0, z, pair_step)

    y_copy(3).wait_recv()
    mine = mine + trecv[0, 0:1, :]
    tsend[1] = jnp.broadcast_to(mine, tsend.shape[1:])
    tensor_copy().start()

    for kb, p in ((0, 0), (0, 1), (1, 1)):
        score_grads(z, kb, p)
    add_query_grads(z, (0,), 0)
    add_query_grads(z, (0, 1), 1)
    for h in range(GROUP):
        dqx[:, h * D:(h + 1) * D] = jnp.transpose(dqt[:, lanes(1 - y, h)] * SCALE).astype(BF16)
    y_copy(4).start()
    for kb in range(2):
        dk, dv = key_value_grads(kb, kb * wide)
        own[kb, 0] = dk
        own[kb, 1] = dv
    for h in range(GROUP):
        dq_ref[:, head_columns(y, h)] = jnp.transpose(dqt[:, lanes(y, h)] * SCALE).astype(BF16)

    def add_arrived(i):
        zs = half - 1 - i
        remote(zsend.at[zs], zrecv.at[zs], zsend_sem.at[zs], zrecv_sem.at[zs], partner).wait_recv()
        own[...] = own[...] + zrecv[zs].astype(F32)
    loop(0, half - 1 - z, add_arrived)
    dkvx[...] = own[1 - y].astype(BF16)
    y_copy(5).start()
    dk_ref[:, column(y)] = own[y, 0].astype(BF16)
    dv_ref[:, column(y)] = own[y, 1].astype(BF16)
    tensor_copy().wait_recv()
    dgate_ref[...] = (1.0 - gate) * (mine + trecv[1, 0:1, :])
    y_copy(4).wait_recv()
    dq_ref[:, pl.ds(pl.multiple_of((1 - y) * GROUP * D, GROUP * D), GROUP * D)] = dqr[...]
    y_copy(5).wait_recv()
    dk_ref[:, column(1 - y)] = dkvr[0]
    dv_ref[:, column(1 - y)] = dkvr[1]

    for i in range(6):
        y_copy(i).wait_send()
    tensor_copy().wait_send()
    loop(z + 1, half, lambda zd: up_copy(me, zd).wait_send())
    loop(z + 1, half, lambda zd: up_copy(partner, zd).wait_send())
    loop(0, z, lambda zz: zgrad_copy(zz).wait_send())


def local(n, queries, keys, values, grad_out, gate_logit, block_ids, block_counts):
    rows, width = queries.shape
    kv_width = keys.shape[1]
    assert kv_width == 2 * D and width == 2 * GROUP * D and n % 2 == 0
    half = n // 2
    wide = GROUP * rows
    vmem = pl.BlockSpec(memory_space=pltpu.VMEM)
    smem = pl.BlockSpec(memory_space=pltpu.SMEM)
    pair = (2, rows, D)
    sem = pltpu.SemaphoreType.DMA
    row = pltpu.VMEM((1, 2 * wide), F32)
    dq, dk, dv, dgate = pl.pallas_call(
        functools.partial(kernel, n),
        out_shape=(
            jax.ShapeDtypeStruct((rows, width), BF16),
            jax.ShapeDtypeStruct((rows, kv_width), BF16),
            jax.ShapeDtypeStruct((rows, kv_width), BF16),
            jax.ShapeDtypeStruct((1, rows), F32),
        ),
        in_specs=[smem, smem, vmem, vmem, vmem, vmem, vmem],
        out_specs=(vmem, vmem, vmem, vmem),
        scratch_shapes=[
            pltpu.VMEM((n,) + pair, BF16),
            pltpu.VMEM(pair, BF16),
            pltpu.VMEM((wide, D), BF16),
            pltpu.VMEM((wide, D), BF16),
            pltpu.VMEM((2 * wide, D), BF16),
            pltpu.VMEM((D, 2 * wide), BF16),
            pltpu.VMEM((2 * wide, D), BF16),
            pltpu.VMEM((D, 2 * wide), BF16),
            pltpu.VMEM((n, rows, 2 * wide), BF16),
            pltpu.VMEM((n, 1, 2 * wide), F32),
            row, row, row, row, row,
            pltpu.VMEM((D, 2 * wide), F32),
            pltpu.VMEM((2,) + pair, F32),
            pltpu.VMEM((2, rows, rows), F32),
            pltpu.VMEM((2 * rows, 2 * wide), BF16),
            pltpu.VMEM((2 * rows, 2 * wide), BF16),
            pltpu.VMEM((half, 2) + pair, BF16),
            pltpu.VMEM((half, 2) + pair, BF16),
            pltpu.VMEM((rows, GROUP * D), BF16),
            pltpu.VMEM((rows, GROUP * D), BF16),
            pltpu.VMEM(pair, BF16),
            pltpu.VMEM(pair, BF16),
            pltpu.VMEM((2, 8, rows), F32),
            pltpu.VMEM((2, 8, rows), F32),
            sem((n,)),
            sem((2, half)),
            sem((half,)),
            sem((half,)),
            sem((6,)),
            sem((6,)),
            sem((2,)),
        ],
        compiler_params=pltpu.CompilerParams(
            collective_id=0, has_side_effects=True, vmem_limit_bytes=62 * 1024 * 1024
        ),
        cost_estimate=pl.CostEstimate(
            flops=12 * n * rows * rows * width,
            bytes_accessed=6 * rows * (width + kv_width),
            transcendentals=n * rows * rows * width // D,
        ),
        name="mod_attention_grads",
    )(block_ids, block_counts, queries, keys, values, grad_out, gate_logit.reshape(1, rows))
    return dq, dk, dv, dgate.reshape(rows)


def solution(mesh):
    in_specs = (
        P(("dp", "seq"), "tensor"),
        P(("dp", "seq"), "tensor"),
        P(("dp", "seq"), "tensor"),
        P(("dp", "seq"), "tensor"),
        P(("dp", "seq")),
        P("dp", None),
        P("dp"),
    )
    out_specs = (
        P(("dp", "seq"), "tensor"),
        P(("dp", "seq"), "tensor"),
        P(("dp", "seq"), "tensor"),
        P(("dp", "seq")),
    )
    return jax.shard_map(
        functools.partial(local, mesh.shape["seq"]),
        mesh=mesh, in_specs=in_specs, out_specs=out_specs, check_vma=False,
    )
```

time: 82.7 us -> 67.4 us (0.81)
  the two profiles are of different devices: /device:TPU:0 before, /device:TPU:12 now
where the time goes in v2:
time: 67.4 us; the launch traced here: 67.2 us
  Pallas kernels  61.1 us (91%)
  local copies, waits for them, and re-layouts  5.42 us (8%)
    pallas_call x1, Pallas kernels, local(): pl.pallas_call(functools.partial(kernel, n), out_shape=(jax.ShapeDtypeStr...  61.1 us
    unnamed x13, local copies, waits for them, and re-layouts  5.42 us

profile of v2, /device:TPU:12, one launch (start us, length us, event | category | flops | bytes accessed | tf_op | source)
XLA Modules:
  0.0 67.2 jit_solution(10281541327939936101)
XLA Ops:
  0.6 0.0 copy-start.2
  0.6 0.7 copy-done.2
  1.3 0.7 copy.11.ids_ref
  2.0 61.1 %mod_attention_grads.1 = (bf16[256,1024]{1,0:T(8,128)(2,1)}, bf16[256,256]{1,0:T(8,128)(2,1)}, bf16[256,256]{1,0:T(8,128)(2,1)}, f32[1,256]{1,0:T(1,128)}) custom-call(s32[8,2]{1,0:T(8,128)} %copy.11.ids_ref, s32[8]{0:T(128)} %counts_ref.1, bf16[256,1024]{1,0:T(8,128)(2,1)} %q_ref.1, bf16[256,256]{1,0:T(8,128)(2,1)} %k_ref.1, bf16[256,256]{1,0:T(8,128)(2,1)} %v_ref.1, ...), custom_call_target="tpu_custom_call" | custom-call | flops 6442450944 | bytes 1966080 | tf_op jit(solution)/shard_map/mod_attention_grads/pallas_call | solution.py:287
  63.1 0.0 copy-start.1
  63.1 1.9 %copy.16 = bf16[256,1024]{1,0:T(8,128)(2,1)} copy(bf16[256,1024]{1,0:T(8,128)(2,1)} %get-tuple-element.16) | data formatting | bytes 1048576
  65.0 0.0 copy-done.1
  65.1 0.0 copy-start
  65.1 0.7 copy.17
  65.7 0.3 copy-done
  66.0 0.0 copy-start.3
  66.0 0.7 copy.18
  66.7 0.0 copy-done.3
  66.7 0.6 copy.19
Async XLA Ops:
  0.6 0.7 %copy-start.2 = (s32[8,2]{0,1:T(2,128)S(1)}, s32[8,2]{0,1:T(2,128)}, u32[]{:S(2)}) copy-start(s32[8,2]{0,1:T(2,128)} %param.12) | copy-start | bytes 196
  63.1 1.9 %copy-start.1 = (bf16[256,256]{1,0:T(8,128)(2,1)S(1)}, bf16[256,256]{1,0:T(8,128)(2,1)}, u32[]{:S(2)}) copy-start(bf16[256,256]{1,0:T(8,128)(2,1)} %get-tuple-element.17) | copy-start | bytes 393220
  65.1 1.0 %copy-start = (bf16[256,256]{1,0:T(8,128)(2,1)S(1)}, bf16[256,256]{1,0:T(8,128)(2,1)}, u32[]{:S(2)}) copy-start(bf16[256,256]{1,0:T(8,128)(2,1)} %get-tuple-element.18) | copy-start | bytes 393220
  66.0 0.7 copy-start.3

commit v3 on v2

--- a/solution.py
+++ b/solution.py
@@ -54,11 +54,25 @@
             (tsend.at[0], trecv.at[0]), (dqx, dqr), (dkvx, dkvr))[i]
         return remote(source, target, y_send_sem.at[i], y_recv_sem.at[i], partner)
 
-    def up_copy(b, zd):
-        return remote(kv.at[b], kv.at[b], up_sem.at[b % 2, zd], kv_sem.at[b], 2 * zd + y)
+    def up_copy(b):
+        return remote(kv.at[b], kv.at[b], up_sem.at[b], kv_sem.at[b], me + 2)
+
+    def pass_up(b):
+        @pl.when(z < half - 1)
+        def _():
+            up_copy(b).start()
+
+    def arrive(b):
+        up_copy(b).wait_recv()
+        pass_up(b)
 
     def zgrad_copy(zz):
-        return remote(zsend.at[zz], zrecv.at[z], zsend_sem.at[zz], zrecv_sem.at[z], 2 * zz + y)
+        return remote(zsend.at[zz], zrecv.at[zz], zsend_sem.at[zz], zrecv_sem.at[zz], me - 2)
+
+    def relay(zz):
+        zgrad_copy(zz).wait_recv()
+        zsend[zz] = (zsend[zz].astype(F32) + zrecv[zz].astype(F32)).astype(BF16)
+        zgrad_copy(zz).start()
 
     def tensor_copy():
         return pltpu.make_async_remote_copy(
@@ -78,18 +92,22 @@
     pl.semaphore_signal(barrier, inc=1, device_id={"seq": partner}, device_id_type=MESH)
     pl.semaphore_signal(barrier, inc=1, device_id={"tensor": 1 - tensor}, device_id_type=MESH)
 
-    def greet(step):
-        other = lax.rem(z + step, half)
-        pl.semaphore_signal(barrier, inc=1, device_id={"seq": 2 * other + y}, device_id_type=MESH)
-    loop(1, half, greet)
+    @pl.when(z > 0)
+    def _():
+        pl.semaphore_signal(barrier, inc=1, device_id={"seq": me - 2}, device_id_type=MESH)
+
+    @pl.when(z < half - 1)
+    def _():
+        pl.semaphore_signal(barrier, inc=1, device_id={"seq": me + 2}, device_id_type=MESH)
 
     kv[me, 0] = k_ref[:, column(y)]
     kv[me, 1] = v_ref[:, column(y)]
     kvx[0] = k_ref[:, column(1 - y)]
     kvx[1] = v_ref[:, column(1 - y)]
-    pl.semaphore_wait(barrier, half + 1)
+    has_before, has_after = (z + half - 1) // half, (2 * half - 2 - z) // half
+    pl.semaphore_wait(barrier, 2 + has_before + has_after)
     y_copy(0).start()
-    loop(z + 1, half, lambda zd: up_copy(me, half + z - zd).start())
+    pass_up(me)
 
     def head_columns(g, h):
         return pl.ds(pl.multiple_of((g * GROUP + h) * D, D), D)
@@ -160,8 +178,15 @@
             exps[b, :, at] = e.astype(BF16)
 
     y_copy(0).wait_recv()
-    loop(z + 1, half, lambda zd: up_copy(partner, half + z - zd).start())
+    pass_up(partner)
     first_pass(me, y, True)
+
+    @pl.when(z > 0)
+    def _():
+        for b in (me - 2, partner - 2):
+            arrive(b)
+            first_pass(b, y, False)
+
     y_copy(1).wait_recv()
     y_copy(2).wait_recv()
     for h in range(GROUP):
@@ -170,12 +195,17 @@
     first_pass(partner, 1 - y, True)
     first_pass(2 * z, 1, False)
 
-    def gather_step(i):
-        b = 2 * z - 1 - i
-        remote(kv.at[b], kv.at[b], up_sem.at[0, 0], kv_sem.at[b], partner).wait_recv()
-        first_pass(b, 0, False)
-        first_pass(b, 1, False)
-    loop(0, 2 * z, gather_step)
+    @pl.when(z > 0)
+    def _():
+        for b in (me - 2, partner - 2):
+            first_pass(b, 1 - y, False)
+
+    def gather_step(k):
+        for b in (me - 2 * k, partner - 2 * k):
+            arrive(b)
+            first_pass(b, 0, False)
+            first_pass(b, 1, False)
+    loop(2, z + 1, gather_step)
 
     sums = []
     for p in range(2):
@@ -224,10 +254,19 @@
             dk, dv = key_value_grads(kb, 0)
             zsend[zz, kb, 0] = dk.astype(BF16)
             zsend[zz, kb, 1] = dv.astype(BF16)
-        zgrad_copy(zz).start()
+
+        @pl.when(z == half - 1)
+        def _():
+            zgrad_copy(zz).start()
+
         for p in range(2):
             add_query_grads(zz, (0, 1), p)
     loop(0, z, pair_step)
+    next_to_last = (z == half - 2) & (z > 0)
+
+    @pl.when(next_to_last)
+    def _():
+        relay(0)
 
     y_copy(3).wait_recv()
     mine = mine + trecv[0, 0:1, :]
@@ -248,11 +287,12 @@
     for h in range(GROUP):
         dq_ref[:, head_columns(y, h)] = jnp.transpose(dqt[:, lanes(y, h)] * SCALE).astype(BF16)
 
-    def add_arrived(i):
-        zs = half - 1 - i
-        remote(zsend.at[zs], zrecv.at[zs], zsend_sem.at[zs], zrecv_sem.at[zs], partner).wait_recv()
-        own[...] = own[...] + zrecv[zs].astype(F32)
-    loop(0, half - 1 - z, add_arrived)
+    @pl.when(z < half - 1)
+    def _():
+        loop(jnp.where(next_to_last, 1, 0), z, relay)
+        zgrad_copy(z).wait_recv()
+        own[...] = own[...] + zrecv[z].astype(F32)
+
     dkvx[...] = own[1 - y].astype(BF16)
     y_copy(5).start()
     dk_ref[:, column(y)] = own[y, 0].astype(BF16)
@@ -268,8 +308,11 @@
     for i in range(6):
         y_copy(i).wait_send()
     tensor_copy().wait_send()
-    loop(z + 1, half, lambda zd: up_copy(me, zd).wait_send())
-    loop(z + 1, half, lambda zd: up_copy(partner, zd).wait_send())
+
+    @pl.when(z < half - 1)
+    def _():
+        loop(0, 2 * z + 2, lambda b: up_copy(b).wait_send())
+
     loop(0, z, lambda zz: zgrad_copy(zz).wait_send())
 
 
@@ -320,7 +363,7 @@
             pltpu.VMEM((2, 8, rows), F32),
             pltpu.VMEM((2, 8, rows), F32),
             sem((n,)),
-            sem((2, half)),
+            sem((n,)),
             sem((half,)),
             sem((half,)),
             sem((6,)),

time: 67.4 us -> 65.9 us (0.978)
  the two profiles are of different devices: /device:TPU:12 before, /device:TPU:0 now
where the time goes in v3:
time: 65.9 us; the launch traced here: 65.7 us
  Pallas kernels  59.6 us (90%)
  local copies, waits for them, and re-layouts  5.42 us (8%)
  between operations  0.66 us (1%)
    pallas_call x1, Pallas kernels, local(): pl.pallas_call(functools.partial(kernel, n), out_shape=(jax.ShapeDtypeStr...  59.6 us
    unnamed x13, local copies, waits for them, and re-layouts  5.42 us

profile of v3, /device:TPU:0, one launch (start us, length us, event | category | flops | bytes accessed | tf_op | source)
XLA Modules:
  0.0 65.7 jit_solution(900499886200380521)
XLA Ops:
  0.6 0.0 copy-start.2
  0.6 0.7 %copy-done.2 = s32[8,2]{0,1:T(2,128)S(1)} copy-done((s32[8,2]{0,1:T(2,128)S(1)}, s32[8,2]{0,1:T(2,128)}, u32[]{:S(2)}) %copy-start.2) | copy-done | bytes 88
  1.3 0.7 %copy.11.ids_ref = s32[8,2]{1,0:T(8,128)} copy(s32[8,2]{0,1:T(2,128)S(1)} %copy-done.2) | data formatting | bytes 128 | tf_op args[5]
  2.0 59.6 %mod_attention_grads.1 = (bf16[256,1024]{1,0:T(8,128)(2,1)}, bf16[256,256]{1,0:T(8,128)(2,1)}, bf16[256,256]{1,0:T(8,128)(2,1)}, f32[1,256]{1,0:T(1,128)}) custom-call(s32[8,2]{1,0:T(8,128)} %copy.11.ids_ref, s32[8]{0:T(128)} %counts_ref.1, bf16[256,1024]{1,0:T(8,128)(2,1)} %q_ref.1, bf16[256,256]{1,0:T(8,128)(2,1)} %k_ref.1, bf16[256,256]{1,0:T(8,128)(2,1)} %v_ref.1, ...), custom_call_target="tpu_custom_call" | custom-call | flops 6442450944 | bytes 1966080 | tf_op jit(solution)/shard_map/mod_attention_grads/pallas_call | solution.py:330
  61.6 0.0 copy-start.1
  61.6 1.9 %copy.16 = bf16[256,1024]{1,0:T(8,128)(2,1)} copy(bf16[256,1024]{1,0:T(8,128)(2,1)} %get-tuple-element.16) | data formatting | bytes 1048576
  63.5 0.0 copy-done.1
  63.5 0.0 copy-start
  63.5 0.7 copy.17
  64.2 0.3 copy-done
  64.5 0.0 copy-start.3
  64.5 0.7 copy.18
  65.1 0.0 copy-done.3
  65.2 0.6 copy.19
Async XLA Ops:
  0.6 0.7 %copy-start.2 = (s32[8,2]{0,1:T(2,128)S(1)}, s32[8,2]{0,1:T(2,128)}, u32[]{:S(2)}) copy-start(s32[8,2]{0,1:T(2,128)} %param.12) | copy-start | bytes 196
  61.6 1.9 %copy-start.1 = (bf16[256,256]{1,0:T(8,128)(2,1)S(1)}, bf16[256,256]{1,0:T(8,128)(2,1)}, u32[]{:S(2)}) copy-start(bf16[256,256]{1,0:T(8,128)(2,1)} %get-tuple-element.17) | copy-start | bytes 393220
  63.5 1.0 %copy-start = (bf16[256,256]{1,0:T(8,128)(2,1)S(1)}, bf16[256,256]{1,0:T(8,128)(2,1)}, u32[]{:S(2)}) copy-start(bf16[256,256]{1,0:T(8,128)(2,1)} %get-tuple-element.18) | copy-start | bytes 393220
  64.5 0.7 %copy-start.3 = (f32[1,256]{1,0:T(1,128)S(1)}, f32[1,256]{1,0:T(1,128)}, u32[]{:S(2)}) copy-start(f32[1,256]{1,0:T(1,128)} %get-tuple-element.11) | copy-start | bytes 3076

commit v4 on v3

--- a/solution.py
+++ b/solution.py
@@ -26,7 +26,7 @@
     n,
     ids_ref, counts_ref, q_ref, k_ref, v_ref, go_ref, gate_ref,
     dq_ref, dk_ref, dv_ref, dgate_ref,
-    kv, kvx, qx, ox, qn, qt, on, ot, exps, block_max, row_max, row_sum, row_dot, delta, factor,
+    kv, kvx, qx, ox, qn, qt, on, ot, exps, block_max, row_max, row_sum, row_out, delta, factor,
     dqt, own, bias, low, scored, zsend, zrecv, dqx, dqr, dkvx, dkvr, tsend, trecv,
     kv_sem, up_sem, zsend_sem, zrecv_sem, y_send_sem, y_recv_sem, t_sem,
 ):
@@ -141,7 +141,7 @@
     live = []
     for p in range(2):
         b = 2 * z + p
-        id0, id1, count = ids_ref[b, 0], ids_ref[b, 1], counts_ref[b]
+        id0, id1, count = ids_ref[0, b], ids_ref[1, b], counts_ref[b]
         key_pos = by_slot(key_row, id0 * BLK, id1 * BLK - BLK) + key_row
         query_pos = by_slot(query_row, id0 * BLK, id1 * BLK - BLK) + query_row
         allowed = ((key_slot < count) & (key_pos <= query_pos)) | (key_row == query_row)
@@ -149,56 +149,66 @@
         live.append(jnp.where(query_slot < count, 1.0, 0.0).astype(F32))
 
     def first_pass(b, p, is_own):
-        keys, values = kv[b, 0], kv[b, 1]
+        keys, values_t = kv[b, 0], jnp.transpose(kv[b, 1])
         shut0 = jnp.where(counts_ref[b] > 0, 0.0, -jnp.inf).astype(F32)
         shut1 = jnp.where(counts_ref[b] > 1, 0.0, -jnp.inf).astype(F32)
         for h in range(GROUP):
-            at = lanes(p, h)
+            at = slice(p * wide + h * rows, p * wide + (h + 1) * rows)
             s = mm(keys, qt[:, at])
             if is_own:
                 s = s + bias[p]
             else:
                 s = jnp.concatenate([s[:BLK] + shut0, s[BLK:] + shut1], axis=0)
-            prob_grads = mm(values, ot[:, at])
             top = jnp.max(s, axis=0, keepdims=True)
             if not is_own:
                 before = row_max[:, at]
                 top = jnp.maximum(before, top)
             e = jnp.exp2((s - top) * EXP2_SCALE)
             total = jnp.sum(e, axis=0, keepdims=True)
-            dot = jnp.sum(e * prob_grads, axis=0, keepdims=True)
+            low_e = e.astype(BF16)
+            weighted = mm(values_t, low_e)
             if not is_own:
                 shrink = jnp.exp2((before - top) * EXP2_SCALE)
                 total = total + row_sum[:, at] * shrink
-                dot = dot + row_dot[:, at] * shrink
+                weighted = weighted + row_out[:, at] * shrink
             row_max[:, at] = top
             row_sum[:, at] = total
-            row_dot[:, at] = dot
+            row_out[:, at] = weighted
             block_max[b, :, at] = top
-            exps[b, :, at] = e.astype(BF16)
+            exps[b, :, at] = low_e
+
+    def for_shard(parity, body):
+        for p in range(2):
+            pl.when(parity == p)(functools.partial(body, p))
 
     y_copy(0).wait_recv()
     pass_up(partner)
-    first_pass(me, y, True)
-
-    @pl.when(z > 0)
-    def _():
+    for_shard(y, lambda p: first_pass(me, p, True))
+
+    def early(p):
         for b in (me - 2, partner - 2):
             arrive(b)
-            first_pass(b, y, False)
-
+            first_pass(b, p, False)
+
+    def late(p):
+        first_pass(partner, p, True)
+
+    def late_before(p):
+        for b in (me - 2, partner - 2):
+            first_pass(b, p, False)
+
+    @pl.when(z > 0)
+    def _():
+        for_shard(y, early)
     y_copy(1).wait_recv()
-    y_copy(2).wait_recv()
     for h in range(GROUP):
         qt[:, lanes(1 - y, h)] = jnp.transpose(qn[lanes(1 - y, h), :])
-        ot[:, lanes(1 - y, h)] = jnp.transpose(on[lanes(1 - y, h), :])
-    first_pass(partner, 1 - y, True)
+    for_shard(1 - y, late)
     first_pass(2 * z, 1, False)
 
     @pl.when(z > 0)
     def _():
-        for b in (me - 2, partner - 2):
-            first_pass(b, 1 - y, False)
+        for_shard(1 - y, late_before)
 
     def gather_step(k):
         for b in (me - 2 * k, partner - 2 * k):
@@ -207,13 +217,17 @@
             first_pass(b, 1, False)
     loop(2, z + 1, gather_step)
 
+    y_copy(2).wait_recv()
+    for h in range(GROUP):
+        ot[:, lanes(1 - y, h)] = jnp.transpose(on[lanes(1 - y, h), :])
     sums = []
     for p in range(2):
         total = jnp.zeros((1, rows), F32)
         for h in range(GROUP):
             at = lanes(p, h)
             inverse = live[p] / row_sum[:, at]
-            rows_delta = row_dot[:, at] * inverse
+            dot = jnp.sum(row_out[:, at] * ot[:, at].astype(F32), axis=0, keepdims=True)
+            rows_delta = dot * inverse
             delta[:, at] = rows_delta
             factor[:, at] = inverse
             total = total + rows_delta
@@ -314,6 +328,22 @@
         loop(0, 2 * z + 2, lambda b: up_copy(b).wait_send())
 
     loop(0, z, lambda zz: zgrad_copy(zz).wait_send())
+
+
+def hand_over(*refs):
+    count = (len(refs) - 1) // 2
+    sems = refs[-1]
+    copies = []
+    for source, target in zip(refs[:count], refs[count:-1]):
+        rows = source.shape[0]
+        step = rows // 4 if rows * source.shape[1] > 2 ** 17 else rows
+        for first in range(0, rows, step):
+            at = pl.ds(first, step)
+            copies.append(pltpu.make_async_copy(source.at[at], target.at[at], sems.at[len(copies)]))
+    for copy in copies:
+        copy.start()
+    for copy in copies:
+        copy.wait()
 
 
 def local(n, queries, keys, values, grad_out, gate_logit, block_ids, block_counts):
@@ -348,7 +378,9 @@
             pltpu.VMEM((D, 2 * wide), BF16),
             pltpu.VMEM((n, rows, 2 * wide), BF16),
             pltpu.VMEM((n, 1, 2 * wide), F32),
-            row, row, row, row, row,
+            row, row,
+            pltpu.VMEM((D, 2 * wide), F32),
+            row, row,
             pltpu.VMEM((D, 2 * wide), F32),
             pltpu.VMEM((2,) + pair, F32),
             pltpu.VMEM((2, rows, rows), F32),
@@ -379,7 +411,17 @@
             transcendentals=n * rows * rows * width // D,
         ),
         name="mod_attention_grads",
-    )(block_ids, block_counts, queries, keys, values, grad_out, gate_logit.reshape(1, rows))
+    )(block_ids.T, block_counts, queries, keys, values, grad_out, gate_logit.reshape(1, rows))
+    results = (dq, dk, dv, dgate)
+    anywhere = pl.BlockSpec(memory_space=pl.ANY)
+    dq, dk, dv, dgate = pl.pallas_call(
+        hand_over,
+        out_shape=tuple(jax.ShapeDtypeStruct(x.shape, x.dtype) for x in results),
+        in_specs=[anywhere] * 4,
+        out_specs=(anywhere,) * 4,
+        scratch_shapes=[sem((7,))],
+        name="hand_over",
+    )(*results)
     return dq, dk, dv, dgate.reshape(rows)
 
 

time: 65.9 us -> 86 us (1.31)
  Pallas kernels: 59.6 us -> 85.1 us
  local copies, waits for them, and re-layouts: 5.42 us -> 0 us
    pallas_call x0 -> x1, Pallas kernels: none -> 25 us  [local(): pl.pallas_call(hand_over, out_shape=tuple((jax.ShapeDtypeStruct(x.shape,...]
    unnamed x13 -> x0, local copies, waits for them, and re-layouts: 5.42 us -> none
where the time goes in v4:
time: 86 us; the launch traced here: 85.9 us
  Pallas kernels  85.1 us (99%)
    pallas_call x1, Pallas kernels, local(): pl.pallas_call(functools.partial(kernel, n), out_shape=(jax.ShapeDtypeStr...  60.1 us
    pallas_call x1, Pallas kernels, local(): pl.pallas_call(hand_over, out_shape=tuple((jax.ShapeDtypeStruct(x.shape,...  25 us

profile of v4, /device:TPU:0, one launch (start us, length us, event | category | flops | bytes accessed | tf_op | source)
XLA Modules:
  0.0 85.9 jit_solution(9913518019802381948)
XLA Ops:
  0.6 60.1 %mod_attention_grads.1 = (bf16[256,1024]{1,0:T(8,128)(2,1)}, bf16[256,256]{1,0:T(8,128)(2,1)}, bf16[256,256]{1,0:T(8,128)(2,1)}, f32[1,256]{1,0:T(1,128)}) custom-call(s32[2,8]{1,0:T(2,128)} %bitcast.3, s32[8]{0:T(128)} %counts_ref.1, bf16[256,1024]{1,0:T(8,128)(2,1)} %q_ref.1, bf16[256,256]{1,0:T(8,128)(2,1)} %k_ref.1, bf16[256,256]{1,0:T(8,128)(2,1)} %v_ref.1, ...), custom_call_target="tpu_custom_call" | custom-call | flops 6442450944 | bytes 1966080 | tf_op jit(solution)/shard_map/mod_attention_grads/pallas_call | solution.py:360
  60.7 25.0 %hand_over.1 = (bf16[256,1024]{1,0:T(8,128)(2,1)}, bf16[256,256]{1,0:T(8,128)(2,1)}, bf16[256,256]{1,0:T(8,128)(2,1)}, f32[1,256]{1,0:T(1,128)}) custom-call(bf16[256,1024]{1,0:T(8,128)(2,1)} %get-tuple-element.12.refs_0_, bf16[256,256]{1,0:T(8,128)(2,1)} %get-tuple-element.13.refs_1_, bf16[256,256]{1,0:T(8,128)(2,1)} %get-tuple-element.14.refs_2_, ...), custom_call_target="tpu_custom_call" | custom-call | tf_op jit(solution)/shard_map/hand_over/pallas_call | solution.py:417

commit v5 on v4

--- a/solution.py
+++ b/solution.py
@@ -66,13 +66,13 @@
         up_copy(b).wait_recv()
         pass_up(b)
 
-    def zgrad_copy(zz):
-        return remote(zsend.at[zz], zrecv.at[zz], zsend_sem.at[zz], zrecv_sem.at[zz], me - 2)
-
-    def relay(zz):
-        zgrad_copy(zz).wait_recv()
-        zsend[zz] = (zsend[zz].astype(F32) + zrecv[zz].astype(F32)).astype(BF16)
-        zgrad_copy(zz).start()
+    def zgrad_copy(b):
+        return remote(zsend.at[b], zrecv.at[b], zsend_sem.at[b], zrecv_sem.at[b], me - 2)
+
+    def relay(b):
+        zgrad_copy(b).wait_recv()
+        zsend[b] = (zsend[b].astype(F32) + zrecv[b].astype(F32)).astype(BF16)
+        zgrad_copy(b).start()
 
     def tensor_copy():
         return pltpu.make_async_remote_copy(
@@ -266,12 +266,9 @@
             for p in range(2):
                 score_grads(zz, kb, p)
             dk, dv = key_value_grads(kb, 0)
-            zsend[zz, kb, 0] = dk.astype(BF16)
-            zsend[zz, kb, 1] = dv.astype(BF16)
-
-        @pl.when(z == half - 1)
-        def _():
-            zgrad_copy(zz).start()
+            zsend[2 * zz + kb, 0] = dk.astype(BF16)
+            zsend[2 * zz + kb, 1] = dv.astype(BF16)
+            pl.when(z == half - 1)(lambda b=2 * zz + kb: zgrad_copy(b).start())
 
         for p in range(2):
             add_query_grads(zz, (0, 1), p)
@@ -281,6 +278,7 @@
     @pl.when(next_to_last)
     def _():
         relay(0)
+        relay(1)
 
     y_copy(3).wait_recv()
     mine = mine + trecv[0, 0:1, :]
@@ -303,9 +301,10 @@
 
     @pl.when(z < half - 1)
     def _():
-        loop(jnp.where(next_to_last, 1, 0), z, relay)
-        zgrad_copy(z).wait_recv()
-        own[...] = own[...] + zrecv[z].astype(F32)
+        loop(jnp.where(next_to_last, 2, 0), 2 * z, relay)
+        for kb in range(2):
+            zgrad_copy(2 * z + kb).wait_recv()
+            own[kb] = own[kb] + zrecv[2 * z + kb].astype(F32)
 
     dkvx[...] = own[1 - y].astype(BF16)
     y_copy(5).start()
@@ -327,23 +326,13 @@
     def _():
         loop(0, 2 * z + 2, lambda b: up_copy(b).wait_send())
 
-    loop(0, z, lambda zz: zgrad_copy(zz).wait_send())
+    loop(0, 2 * z, lambda b: zgrad_copy(b).wait_send())
 
 
 def hand_over(*refs):
-    count = (len(refs) - 1) // 2
-    sems = refs[-1]
-    copies = []
-    for source, target in zip(refs[:count], refs[count:-1]):
-        rows = source.shape[0]
-        step = rows // 4 if rows * source.shape[1] > 2 ** 17 else rows
-        for first in range(0, rows, step):
-            at = pl.ds(first, step)
-            copies.append(pltpu.make_async_copy(source.at[at], target.at[at], sems.at[len(copies)]))
-    for copy in copies:
-        copy.start()
-    for copy in copies:
-        copy.wait()
+    count = len(refs) // 2
+    for source, target in zip(refs[:count], refs[count:]):
+        target[...] = source[...]
 
 
 def local(n, queries, keys, values, grad_out, gate_logit, block_ids, block_counts):
@@ -386,8 +375,8 @@
             pltpu.VMEM((2, rows, rows), F32),
             pltpu.VMEM((2 * rows, 2 * wide), BF16),
             pltpu.VMEM((2 * rows, 2 * wide), BF16),
-            pltpu.VMEM((half, 2) + pair, BF16),
-            pltpu.VMEM((half, 2) + pair, BF16),
+            pltpu.VMEM((n,) + pair, BF16),
+            pltpu.VMEM((n,) + pair, BF16),
             pltpu.VMEM((rows, GROUP * D), BF16),
             pltpu.VMEM((rows, GROUP * D), BF16),
             pltpu.VMEM(pair, BF16),
@@ -396,8 +385,8 @@
             pltpu.VMEM((2, 8, rows), F32),
             sem((n,)),
             sem((n,)),
-            sem((half,)),
-            sem((half,)),
+            sem((n,)),
+            sem((n,)),
             sem((6,)),
             sem((6,)),
             sem((2,)),
@@ -413,13 +402,11 @@
         name="mod_attention_grads",
     )(block_ids.T, block_counts, queries, keys, values, grad_out, gate_logit.reshape(1, rows))
     results = (dq, dk, dv, dgate)
-    anywhere = pl.BlockSpec(memory_space=pl.ANY)
     dq, dk, dv, dgate = pl.pallas_call(
         hand_over,
         out_shape=tuple(jax.ShapeDtypeStruct(x.shape, x.dtype) for x in results),
-        in_specs=[anywhere] * 4,
-        out_specs=(anywhere,) * 4,
-        scratch_shapes=[sem((7,))],
+        in_specs=[vmem] * 4,
+        out_specs=(vmem,) * 4,
         name="hand_over",
     )(*results)
     return dq, dk, dv, dgate.reshape(rows)

time: 86 us -> 58.1 us (0.68)
  Pallas kernels: 85.1 us -> 57.3 us
    pallas_call x1, Pallas kernels: 25 us -> 2.02 us  [local(): pl.pallas_call(hand_over, out_shape=tuple((jax.ShapeDtypeStruct(x.shape,...]
    pallas_call x1, Pallas kernels: 60.1 us -> 55.3 us  [local(): pl.pallas_call(functools.partial(kernel, n), out_shape=(jax.ShapeDtypeStr...]
where the time goes in v5:
time: 58.1 us; the launch traced here: 58 us
  Pallas kernels  57.3 us (99%)
  between operations  0.64 us (1%)
    pallas_call x1, Pallas kernels, local(): pl.pallas_call(functools.partial(kernel, n), out_shape=(jax.ShapeDtypeStr...  55.3 us
    pallas_call x1, Pallas kernels, local(): pl.pallas_call(hand_over, out_shape=tuple((jax.ShapeDtypeStruct(x.shape,...  2.02 us

profile of v5, /device:TPU:0, one launch (start us, length us, event | category | flops | bytes accessed | tf_op | source)
XLA Modules:
  0.0 58.0 jit_solution(6679024075995890933)
XLA Ops:
  0.6 55.3 %mod_attention_grads.1 = (bf16[256,1024]{1,0:T(8,128)(2,1)}, bf16[256,256]{1,0:T(8,128)(2,1)}, bf16[256,256]{1,0:T(8,128)(2,1)}, f32[1,256]{1,0:T(1,128)}) custom-call(s32[2,8]{1,0:T(2,128)} %bitcast.3, s32[8]{0:T(128)} %counts_ref.1, bf16[256,1024]{1,0:T(8,128)(2,1)} %q_ref.1, bf16[256,256]{1,0:T(8,128)(2,1)} %k_ref.1, bf16[256,256]{1,0:T(8,128)(2,1)} %v_ref.1, ...), custom_call_target="tpu_custom_call" | custom-call | flops 6442450944 | bytes 1966080 | tf_op jit(solution)/shard_map/mod_attention_grads/pallas_call | solution.py:349
  55.9 2.0 %hand_over.1 = (bf16[256,1024]{1,0:T(8,128)(2,1)}, bf16[256,256]{1,0:T(8,128)(2,1)}, bf16[256,256]{1,0:T(8,128)(2,1)}, f32[1,256]{1,0:T(1,128)}) custom-call(bf16[256,1024]{1,0:T(8,128)(2,1)} %get-tuple-element.12.refs_0_, bf16[256,256]{1,0:T(8,128)(2,1)} %get-tuple-element.13.refs_1_, bf16[256,256]{1,0:T(8,128)(2,1)} %get-tuple-element.14.refs_2_, ...), custom_call_target="tpu_custom_call" | custom-call | tf_op jit(solution)/shard_map/hand_over/pallas_call | solution.py:405
